TPU v7x, 32 devices: a whole 2x2x4 slice. The times are simulated.
32 devices in a mesh: nodes: 8 (over z, y), rep: 4 (over x, core).
Axes of the slice: x: 2, y: 2, z: 4, core: 2. Of those that a mesh axis runs over, the one named last changes fastest.
Arguments:
- queries: bfloat16 [4, 4096, 1024], P('rep', 'nodes'), may hold values from -9 to 9
- keys: bfloat16 [4, 4096, 1024], P('rep', 'nodes'), may hold values from -9 to 9
- values: bfloat16 [4, 4096, 1024], P('rep', 'nodes'), may hold values from -6 to 6
- grad_out: bfloat16 [4, 4096, 1024], P('rep', 'nodes'), may hold values from -6 to 6
- w_out: bfloat16 [1024, 1024], replicated, may hold values from -0.1875 to 0.1875
- cluster_id: int32 [4, 4096], P('rep', 'nodes'), may hold values from 0 to 31, as said below
Outputs:
- grad_queries: bfloat16 [4, 4096, 1024], P('rep', 'nodes')
- grad_keys: bfloat16 [4, 4096, 1024], P('rep', 'nodes')
- grad_values: bfloat16 [4, 4096, 1024], P('rep', 'nodes')
- grad_w_out: float32 [1024, 1024], P('nodes')
Inputs may be any that keep to these rules, and one draw needn't show every extreme that they name: `cluster_id`: cluster c of a window is owned by index c // 4 of the nodes axis. The 512 nodes of one device name clusters of every owner, exactly 64 nodes for each owner. Clusters differ in size and may be empty.
All inputs are finite; a program needn't handle non-finite values.
Results may differ from a plain program's by a relative error of at most 0.013.
The roundings to bfloat16 on the way count: a program that leaves them out, or rounds other values in their place, can miss the bound.
Values may be sent and summed in bfloat16 or wider, within the bound.
A program may use at most 128 MiB of HBM per device.

v0:
```python
import functools
import math

import jax
import jax.numpy as jnp
from jax import lax
from jax.experimental import pallas as pl
from jax.experimental.pallas import tpu as pltpu
from jax.sharding import PartitionSpec as P

HEAD_DIM = 128
CL_DEV = 4
GROUP_HEADS = 2
TAG_LANES = 128
MESH = pl.DeviceIdType.MESH


big_negative = -1e30


def head_grads(query_rows, key_rows, value_rows, grad_rows, tag_rows, score_scale):
    scores = (
        lax.dot_general(
            query_rows, key_rows, (((1,), (1,)), ((), ())), preferred_element_type=jnp.float32
        )
        * score_scale
    )
    allowed = (tag_rows[:, None] == tag_rows[None, :]) & (tag_rows[None, :] > 0)
    scores = jnp.where(allowed, scores, big_negative)
    highest = jnp.max(scores, axis=1, keepdims=True)
    weights = jnp.exp(scores - highest)
    softmax_rows = weights / jnp.sum(weights, axis=1, keepdims=True)
    softmax_low = softmax_rows.astype(jnp.bfloat16)
    attended = jnp.dot(softmax_low, value_rows, preferred_element_type=jnp.float32).astype(
        jnp.bfloat16
    )
    delta_rows = jnp.sum(
        grad_rows.astype(jnp.float32) * attended.astype(jnp.float32), axis=1, keepdims=True
    )
    grad_softmax = lax.dot_general(
        grad_rows, value_rows, (((1,), (1,)), ((), ())), preferred_element_type=jnp.float32
    )
    grad_scores = (softmax_rows * (grad_softmax - delta_rows) * score_scale).astype(jnp.bfloat16)
    grad_query = jnp.dot(grad_scores, key_rows, preferred_element_type=jnp.float32).astype(
        jnp.bfloat16
    )
    grad_key = lax.dot_general(
        grad_scores, query_rows, (((0,), (0,)), ((), ())), preferred_element_type=jnp.float32
    ).astype(jnp.bfloat16)
    grad_value = lax.dot_general(
        softmax_low, grad_rows, (((0,), (0,)), ((), ())), preferred_element_type=jnp.float32
    ).astype(jnp.bfloat16)
    return (grad_query, grad_key, grad_value, attended)


def all_heads(query_all, key_all, value_all, grad_all, tag_all, score_scale):
    collected = [[], [], [], []]
    for head_index in range(query_all.shape[1]):
        outputs = head_grads(
            query_all[:, head_index],
            key_all[:, head_index],
            value_all[:, head_index],
            grad_all[:, head_index],
            tag_all[:, head_index],
            score_scale,
        )
        for member in range(4):
            collected[member].append(outputs[member])
    return tuple((jnp.stack(pieces_list, axis=1) for pieces_list in collected))


def local_plain(queries, keys, values, grad_out, w_out, cluster_id):
    node_count = lax.axis_size("nodes")
    rows_here = queries.shape[1]
    model_width = queries.shape[2]
    head_count = model_width // HEAD_DIM
    bucket = rows_here // node_count
    buffer_rows = node_count * bucket
    head_shape = (buffer_rows, head_count, HEAD_DIM)
    score_scale = 1.0 / math.sqrt(HEAD_DIM)
    norm_factor = 1.0 / math.sqrt(lax.axis_size("rep") * node_count * rows_here)
    cluster_ids = cluster_id[0]
    owner_ids = cluster_ids // CL_DEV
    sub_ids = cluster_ids - owner_ids * CL_DEV
    owner_table = (owner_ids[:, None] == jnp.arange(node_count, dtype=jnp.int32)[None, :]).astype(
        jnp.float32
    )
    row_numbers = jnp.arange(rows_here, dtype=jnp.int32)
    earlier = (row_numbers[:, None] > row_numbers[None, :]).astype(jnp.float32)
    before = jnp.dot(earlier, owner_table, precision=lax.Precision.HIGHEST)
    rank_in_bucket = jnp.sum(before * owner_table, axis=1).astype(jnp.int32)
    slot_index = owner_ids * bucket + rank_in_bucket

    def to_buffer(rows):
        return jnp.zeros((buffer_rows,) + rows.shape[1:], rows.dtype).at[slot_index].set(rows)

    tag_column = to_buffer((sub_ids + 1).astype(jnp.bfloat16))
    tag_grid = jnp.broadcast_to(tag_column[:, None], (buffer_rows, head_count))
    query_local = queries[0]
    key_local = keys[0]
    value_local = values[0]
    grad_local = grad_out[0]
    arrived = (
        lax.all_to_all(to_buffer(query_local), "nodes", split_axis=0, concat_axis=0, tiled=True),
        lax.all_to_all(to_buffer(key_local), "nodes", split_axis=0, concat_axis=0, tiled=True),
        lax.all_to_all(to_buffer(value_local), "nodes", split_axis=0, concat_axis=0, tiled=True),
        lax.all_to_all(to_buffer(grad_local), "nodes", split_axis=0, concat_axis=0, tiled=True),
        lax.all_to_all(tag_grid, "nodes", split_axis=0, concat_axis=0, tiled=True),
    )
    query_recv, key_recv, value_recv, grad_recv, tag_recv = arrived
    grad_attended = jnp.dot(grad_recv, w_out, preferred_element_type=jnp.float32).astype(
        jnp.bfloat16
    )
    results = all_heads(
        query_recv.reshape(head_shape),
        key_recv.reshape(head_shape),
        value_recv.reshape(head_shape),
        grad_attended.reshape(head_shape),
        tag_recv,
        score_scale,
    )
    flattened = [result.reshape(buffer_rows, model_width) for result in results]
    returned = (
        lax.all_to_all(flattened[0], "nodes", split_axis=0, concat_axis=0, tiled=True),
        lax.all_to_all(flattened[1], "nodes", split_axis=0, concat_axis=0, tiled=True),
        lax.all_to_all(flattened[2], "nodes", split_axis=0, concat_axis=0, tiled=True),
    )
    grad_query = returned[0][slot_index]
    grad_key = returned[1][slot_index]
    grad_value = returned[2][slot_index]
    attended_rows = flattened[3]
    row_share = lax.psum_scatter(
        lax.dot_general(
            grad_recv, attended_rows, (((0,), (0,)), ((), ())), preferred_element_type=jnp.float32
        )
        * norm_factor,
        "nodes",
        scatter_dimension=0,
        tiled=True,
    )
    grad_weight = lax.psum(row_share.astype(jnp.bfloat16), "rep").astype(jnp.float32)
    return (grad_query[None], grad_key[None], grad_value[None], grad_weight)


def dot_rows(a, b):
    return lax.dot_general(a, b, (((0,), (0,)), ((), ())), preferred_element_type=jnp.float32)


def dot_lanes(a, b):
    return lax.dot_general(a, b, (((1,), (1,)), ((), ())), preferred_element_type=jnp.float32)


def dot(a, b):
    return jnp.dot(a, b, preferred_element_type=jnp.float32)


def layer_kernel(
    nn, rr, groups, norm_factor,
    slot_row, slot_col, tags, q_ref, k_ref, v_ref, g_ref, w_ref,
    dq_ref, dk_ref, dv_ref, dw_ref,
    perm, unperm, gsend, grecv, send, recv, ga, bias, att, bsend, brecv,
    wsend, wrecv, nsend, nrecv, fsend, frecv,
    g_ss, g_rs, in_ss, in_rs, b_ss, b_rs, w_ss, w_rs, n_ss, n_rs, f_ss, f_rs,
):
    low = jnp.bfloat16
    me = lax.axis_index("nodes")
    mr = lax.axis_index("rep")
    rows, width = q_ref.shape
    bucket = rows // nn
    gcols = width // groups
    seg = width // (nn * rr)
    scale = 1.0 / math.sqrt(HEAD_DIM)

    def ahead(d):
        return lax.rem(me + d, nn)

    def behind(d):
        return lax.rem(me + nn - d, nn)

    def rep_ahead(d):
        return lax.rem(mr + d, rr)

    def rep_behind(d):
        return lax.rem(mr + rr - d, rr)

    def g_copy(d, slot):
        peer = ahead(d)
        return pltpu.make_async_remote_copy(
            src_ref=gsend.at[peer], dst_ref=grecv.at[slot], send_sem=g_ss.at[d],
            recv_sem=g_rs.at[d], device_id={"nodes": peer}, device_id_type=MESH)

    def in_copy(g, d, slot):
        peer = ahead(d)
        return pltpu.make_async_remote_copy(
            src_ref=send.at[g, peer], dst_ref=recv.at[g, slot], send_sem=in_ss.at[g, d],
            recv_sem=in_rs.at[g, d], device_id={"nodes": peer}, device_id_type=MESH)

    def back_copy(g, d, slot):
        peer = ahead(d)
        return pltpu.make_async_remote_copy(
            src_ref=bsend.at[g, peer], dst_ref=brecv.at[g, slot], send_sem=b_ss.at[g, d],
            recv_sem=b_rs.at[g, d], device_id={"nodes": peer}, device_id_type=MESH)

    def w_copy(g, d, slot):
        peer = rep_ahead(d)
        return pltpu.make_async_remote_copy(
            src_ref=wsend.at[g, peer], dst_ref=wrecv.at[g, slot], send_sem=w_ss.at[g, d],
            recv_sem=w_rs.at[g, d], device_id={"rep": peer}, device_id_type=MESH)

    def n_copy(g, d, slot):
        peer = ahead(d)
        return pltpu.make_async_remote_copy(
            src_ref=nsend.at[g, peer], dst_ref=nrecv.at[g, slot], send_sem=n_ss.at[g, d],
            recv_sem=n_rs.at[g, d], device_id={"nodes": peer}, device_id_type=MESH)

    def f_copy(d, slot):
        peer = rep_ahead(d)
        return pltpu.make_async_remote_copy(
            src_ref=fsend, dst_ref=frecv.at[slot], send_sem=f_ss.at[d],
            recv_sem=f_rs.at[d], device_id={"rep": peer}, device_id_type=MESH)

    def each(count, act):
        def step(d, carry):
            act(d)
            return carry

        lax.fori_loop(1, count, step, 0)

    barrier = pltpu.get_barrier_semaphore()
    for d in range(1, nn):
        pl.semaphore_signal(barrier, inc=1, device_id={"nodes": ahead(d)}, device_id_type=MESH)
    for d in range(1, rr):
        pl.semaphore_signal(barrier, inc=1, device_id={"rep": rep_ahead(d)}, device_id_type=MESH)

    perm[...] = (
        lax.broadcasted_iota(jnp.int32, (rows, rows), 0) == slot_row[...]
    ).astype(jnp.float32).astype(low)
    unperm[...] = (
        lax.broadcasted_iota(jnp.int32, (rows, rows), 1) == slot_col[...]
    ).astype(jnp.float32).astype(low)

    gsend[:, :, :width] = dot(perm[...], g_ref[...]).astype(low).reshape(nn, bucket, width)
    gsend[:, :, width:] = dot(perm[...], tags[...]).astype(low).reshape(nn, bucket, TAG_LANES)
    pl.semaphore_wait(barrier, nn + rr - 2)
    each(nn, lambda d: g_copy(d, me).start())
    grecv[me] = gsend[me]

    def perm_send(g):
        cols = pl.ds(pl.multiple_of(g * gcols, HEAD_DIM), gcols)
        for i, ref in enumerate((q_ref, k_ref, v_ref)):
            send[g, :, i] = dot(perm[...], ref[:, cols]).astype(low).reshape(nn, bucket, gcols)
        each(nn, lambda d: in_copy(g, d, me).start())
        recv[g, me] = send[g, me]

    perm_send(0)
    if groups > 1:
        perm_send(1)

    each(nn, lambda d: g_copy(d, behind(d)).wait_recv())
    ga[...] = dot(grecv[:, :, :width].reshape(rows, width), w_ref[...]).astype(low)
    tag_rows = grecv[:, :, width:].reshape(rows, TAG_LANES)
    bias[...] = jnp.where(dot_lanes(tag_rows, tag_rows) > 0.5, 0.0, big_negative)

    def rep_sum(g):
        each(rr, lambda d: w_copy(g, d, rep_behind(d)).wait_recv())
        total = wsend[g, mr].astype(jnp.float32)
        for d in range(1, rr):
            total = total + wrecv[g, rep_behind(d)].astype(jnp.float32)
        nsend[g] = total.astype(low)
        each(nn, lambda d: n_copy(g, d, me).start())

    def node_sum(g):
        each(nn, lambda d: n_copy(g, d, behind(d)).wait_recv())
        total = nsend[g, me].astype(jnp.float32)
        for d in range(1, nn):
            total = total + nrecv[g, behind(d)].astype(jnp.float32)
        cols = pl.ds(pl.multiple_of(g * gcols, HEAD_DIM), gcols)
        fsend[:, cols] = total.astype(low)

    def put_back(g):
        each(nn, lambda d: back_copy(g, d, behind(d)).wait_recv())
        cols = pl.ds(pl.multiple_of(g * gcols, HEAD_DIM), gcols)
        for i, ref in enumerate((dq_ref, dk_ref, dv_ref)):
            ref[:, cols] = dot(unperm[...], brecv[g, :, i].reshape(rows, gcols)).astype(low)

    def group_step(g, carry):
        @pl.when(g + 2 < groups)
        def _():
            perm_send(g + 2)

        each(nn, lambda d: in_copy(g, d, behind(d)).wait_recv())
        for h in range(gcols // HEAD_DIM):
            hc = slice(h * HEAD_DIM, (h + 1) * HEAD_DIM)
            q = recv[g, :, 0, :, hc].reshape(rows, HEAD_DIM)
            k = recv[g, :, 1, :, hc].reshape(rows, HEAD_DIM)
            v = recv[g, :, 2, :, hc].reshape(rows, HEAD_DIM)
            gr = ga[:, pl.ds(pl.multiple_of(g * gcols + h * HEAD_DIM, HEAD_DIM), HEAD_DIM)]
            scores = dot_lanes(q, k) * scale + bias[...]
            weights = jnp.exp(scores - jnp.max(scores, axis=1, keepdims=True))
            probs = weights / jnp.sum(weights, axis=1, keepdims=True)
            probs_low = probs.astype(low)
            attended = dot(probs_low, v).astype(low)
            att[:, hc] = attended
            delta = jnp.sum(
                gr.astype(jnp.float32) * attended.astype(jnp.float32), axis=1, keepdims=True)
            ds = (probs * (dot_lanes(gr, v) - delta) * scale).astype(low)
            shape = (nn, bucket, HEAD_DIM)
            bsend[g, :, 0, :, hc] = dot(ds, k).astype(low).reshape(shape)
            bsend[g, :, 1, :, hc] = dot_rows(ds, q).astype(low).reshape(shape)
            bsend[g, :, 2, :, hc] = dot_rows(probs_low, gr).astype(low).reshape(shape)
        each(nn, lambda d: back_copy(g, d, me).start())
        brecv[g, me] = bsend[g, me]
        share = dot_rows(grecv[:, :, :width].reshape(rows, width), att[...]) * norm_factor
        share = share.astype(low).reshape(nn, rr, seg, gcols)
        for r in range(rr):
            wsend[g, r] = share[:, r]
        each(rr, lambda d: w_copy(g, d, mr).start())

        @pl.when(g >= 1)
        def _():
            rep_sum(g - 1)

        @pl.when(g >= 2)
        def _():
            node_sum(g - 2)

        return carry

    lax.fori_loop(0, groups, group_step, 0)
    rep_sum(groups - 1)

    def early(g, carry):
        put_back(g)
        return carry

    lax.fori_loop(0, groups - 1, early, 0)
    if groups > 1:
        node_sum(groups - 2)
    node_sum(groups - 1)
    each(rr, lambda d: f_copy(d, mr).start())
    put_back(groups - 1)
    frecv[mr] = fsend[...]
    each(rr, lambda d: f_copy(d, rep_behind(d)).wait_recv())
    dw_ref[...] = frecv[...].reshape(rr * seg, width).astype(jnp.float32)

    each(nn, lambda d: g_copy(d, me).wait_send())

    def drain(g, carry):
        each(nn, lambda d: in_copy(g, d, me).wait_send())
        each(nn, lambda d: back_copy(g, d, me).wait_send())
        each(nn, lambda d: n_copy(g, d, me).wait_send())
        each(rr, lambda d: w_copy(g, d, mr).wait_send())
        return carry

    lax.fori_loop(0, groups, drain, 0)
    each(rr, lambda d: f_copy(d, mr).wait_send())


def local_kernel(queries, keys, values, grad_out, w_out, cluster_id):
    nn = lax.axis_size("nodes")
    rr = lax.axis_size("rep")
    rows, width = queries.shape[1:]
    bucket = rows // nn
    groups = width // HEAD_DIM // GROUP_HEADS
    gcols = width // groups
    seg = width // (nn * rr)
    norm_factor = 1.0 / math.sqrt(rr * nn * rows)
    low = jnp.bfloat16
    ids = cluster_id[0]
    owners = ids // CL_DEV
    subs = ids - owners * CL_DEV
    table = owners[:, None] == jnp.arange(nn, dtype=jnp.int32)[None, :]
    number = jnp.arange(rows, dtype=jnp.int32)
    earlier = (number[:, None] > number[None, :]).astype(low)
    before = jnp.dot(earlier, table.astype(low), preferred_element_type=jnp.float32)
    rank = jnp.sum(jnp.where(table, before, 0.0), axis=1).astype(jnp.int32)
    slot = owners * bucket + rank
    tags = (subs[:, None] == jnp.arange(TAG_LANES, dtype=jnp.int32)[None, :]).astype(low)
    vmem = pl.BlockSpec(memory_space=pltpu.VMEM)
    dma = pltpu.SemaphoreType.DMA
    ext = width + TAG_LANES
    outs = pl.pallas_call(
        functools.partial(layer_kernel, nn, rr, groups, norm_factor),
        out_shape=[jax.ShapeDtypeStruct((rows, width), low)] * 3
        + [jax.ShapeDtypeStruct((rr * seg, width), jnp.float32)],
        in_specs=[vmem] * 8,
        out_specs=[vmem] * 4,
        scratch_shapes=[
            pltpu.VMEM((rows, rows), low),
            pltpu.VMEM((rows, rows), low),
            pltpu.VMEM((nn, bucket, ext), low),
            pltpu.VMEM((nn, bucket, ext), low),
            pltpu.VMEM((groups, nn, 3, bucket, gcols), low),
            pltpu.VMEM((groups, nn, 3, bucket, gcols), low),
            pltpu.VMEM((rows, width), low),
            pltpu.VMEM((rows, rows), jnp.float32),
            pltpu.VMEM((rows, gcols), low),
            pltpu.VMEM((groups, nn, 3, bucket, gcols), low),
            pltpu.VMEM((groups, nn, 3, bucket, gcols), low),
            pltpu.VMEM((groups, rr, nn, seg, gcols), low),
            pltpu.VMEM((groups, rr, nn, seg, gcols), low),
            pltpu.VMEM((groups, nn, seg, gcols), low),
            pltpu.VMEM((groups, nn, seg, gcols), low),
            pltpu.VMEM((seg, width), low),
            pltpu.VMEM((rr, seg, width), low),
            dma((nn,)), dma((nn,)),
            dma((groups, nn)), dma((groups, nn)),
            dma((groups, nn)), dma((groups, nn)),
            dma((groups, rr)), dma((groups, rr)),
            dma((groups, nn)), dma((groups, nn)),
            dma((rr,)), dma((rr,)),
        ],
        compiler_params=pltpu.CompilerParams(
            collective_id=0, has_side_effects=True, vmem_limit_bytes=56 * 1024 * 1024
        ),
    )(slot[None, :], slot[:, None], tags, queries[0], keys[0], values[0], grad_out[0], w_out)
    return (outs[0][None], outs[1][None], outs[2][None], outs[3])


def local(queries, keys, values, grad_out, w_out, cluster_id):
    nn, rr = lax.axis_size("nodes"), lax.axis_size("rep")
    rows, width = queries.shape[1:]
    heads = width // HEAD_DIM
    fits = (
        rows % (16 * nn) == 0 and width % (16 * nn * rr) == 0 and heads % GROUP_HEADS == 0
        and CL_DEV <= TAG_LANES and nn > 1 and rr > 1
    )
    chosen = local_kernel if fits else local_plain
    return chosen(queries, keys, values, grad_out, w_out, cluster_id)


def solution(mesh):
    in_specs = (
        P("rep", "nodes", None),
        P("rep", "nodes", None),
        P("rep", "nodes", None),
        P("rep", "nodes", None),
        P(),
        P("rep", "nodes"),
    )
    out_specs = (
        P("rep", "nodes", None),
        P("rep", "nodes", None),
        P("rep", "nodes", None),
        P("nodes", None),
    )
    return jax.shard_map(local, mesh=mesh, in_specs=in_specs, out_specs=out_specs, check_vma=False)
```

profile of v0, /device:TPU:1, one launch (start us, length us, event | category | flops | bytes accessed | tf_op | source)
XLA Modules:
  0.0 201.6 jit_solution(5635046564527986762)
XLA Ops:
  0.6 0.7 multiply_subtract_fusion
  1.3 0.3 fusion
  1.6 1.3 multiply_add_fusion.slot_row
  2.9 0.8 fusion.5.tags
  3.7 0.1 copy.20
  3.8 0.8 copy.15
  4.7 0.9 fusion.3.slot_col
  5.5 190.9 %shard_map.93 = (bf16[512,1024]{1,0:T(8,128)(2,1)}, bf16[512,1024]{1,0:T(8,128)(2,1)}, bf16[512,1024]{1,0:T(8,128)(2,1)}, f32[128,1024]{1,0:T(8,128)}) custom-call(s32[1,512]{1,0:T(1,128)} %multiply_add_fusion.slot_row, s32[512,1]{1,0:T(8,128)} %fusion.3.slot_col, bf16[512,128]{1,0:T(8,128)(2,1)} %fusion.5.tags, bf16[512,1024]{1,0:T(8,128)(2,1)} %bitcast.14, ...), custom_call_target="tpu_custom_call" | custom-call | tf_op jit(solution)/shard_map/pallas_call | solution.py:382
  196.4 0.0 copy-start.1
  196.4 0.0 copy-start
  196.5 2.4 %copy.25 = bf16[1,512,1024]{2,1,0:T(8,128)(2,1)} copy(bf16[1,512,1024]{2,1,0:T(8,128)(2,1)} %bitcast.13) | data formatting | bytes 2097152
  198.9 0.0 copy-done.1
  198.9 0.0 copy-start.2
  198.9 1.0 copy.26
  199.8 0.0 copy-done
  199.8 1.0 copy.27
  200.8 0.0 copy-done.2
  200.8 0.8 copy.28
  (1 shorter events, 0.0 us)
Async XLA Ops:
  196.4 2.4 %copy-start.1 = (bf16[512,1024]{1,0:T(8,128)(2,1)S(1)}, bf16[512,1024]{1,0:T(8,128)(2,1)}, u32[]{:S(2)}) copy-start(bf16[512,1024]{1,0:T(8,128)(2,1)} %get-tuple-element.9) | copy-start | bytes 3145732
  196.4 3.4 %copy-start = (bf16[512,1024]{1,0:T(8,128)(2,1)S(1)}, bf16[512,1024]{1,0:T(8,128)(2,1)}, u32[]{:S(2)}) copy-start(bf16[512,1024]{1,0:T(8,128)(2,1)} %get-tuple-element.10) | copy-start | bytes 3145732
  198.9 1.9 copy-start.2
where the time goes:
time: 202 us
  Pallas kernels  191 us (95%)
  local copies, waits for them, and re-layouts  6.12 us (3%)
  other arithmetic  3.64 us (2%)
    pallas_call x1, Pallas kernels, local_kernel(): pl.pallas_call(functools.partial(layer_kernel, nn, rr, groups, norm_facto...  191 us
    unnamed x10, local copies, waits for them, and re-layouts  5.15 us

commit v1 on v0

--- a/solution.py
+++ b/solution.py
@@ -1,4 +1,5 @@
 import functools
+import itertools
 import math
 
 import jax
@@ -10,7 +11,8 @@
 
 HEAD_DIM = 128
 CL_DEV = 4
-GROUP_HEADS = 2
+GROUP_HEADS = 4
+TAG_ROWS = 16
 TAG_LANES = 128
 MESH = pl.DeviceIdType.MESH
 
@@ -156,11 +158,11 @@
 
 def layer_kernel(
     nn, rr, groups, norm_factor,
-    slot_row, slot_col, tags, q_ref, k_ref, v_ref, g_ref, w_ref,
+    ids_ref, q_ref, k_ref, v_ref, g_ref, w_ref,
     dq_ref, dk_ref, dv_ref, dw_ref,
-    perm, unperm, gsend, grecv, send, recv, ga, bias, att, bsend, brecv,
+    perm, unperm, gsend, grecv, tsend, trecv, send, recv, ga, bias, att, bsend, brecv,
     wsend, wrecv, nsend, nrecv, fsend, frecv,
-    g_ss, g_rs, in_ss, in_rs, b_ss, b_rs, w_ss, w_rs, n_ss, n_rs, f_ss, f_rs,
+    g_ss, g_rs, t_ss, t_rs, in_ss, in_rs, b_ss, b_rs, w_ss, w_rs, n_ss, n_rs, f_ss, f_rs,
 ):
     low = jnp.bfloat16
     me = lax.axis_index("nodes")
@@ -171,11 +173,23 @@
     seg = width // (nn * rr)
     scale = 1.0 / math.sqrt(HEAD_DIM)
 
+    paired = nn & (nn - 1) == 0
+    near, far = list(range(1, nn // 2)), list(range(max(nn // 2, 1), nn))
+    order = [d for two in itertools.zip_longest(far, near) for d in two if d is not None]
+
+    def flipped(d):
+        peer, bit = me, 1
+        while bit < nn:
+            if d & bit:
+                peer = peer + bit - 2 * bit * lax.rem(me // bit, 2)
+            bit *= 2
+        return peer
+
     def ahead(d):
-        return lax.rem(me + d, nn)
+        return flipped(d) if paired else lax.rem(me + d, nn)
 
     def behind(d):
-        return lax.rem(me + nn - d, nn)
+        return flipped(d) if paired else lax.rem(me + nn - d, nn)
 
     def rep_ahead(d):
         return lax.rem(mr + d, rr)
@@ -188,6 +202,12 @@
         return pltpu.make_async_remote_copy(
             src_ref=gsend.at[peer], dst_ref=grecv.at[slot], send_sem=g_ss.at[d],
             recv_sem=g_rs.at[d], device_id={"nodes": peer}, device_id_type=MESH)
+
+    def t_copy(d, slot):
+        peer = ahead(d)
+        return pltpu.make_async_remote_copy(
+            src_ref=tsend.at[peer], dst_ref=trecv.at[slot], send_sem=t_ss.at[d],
+            recv_sem=t_rs.at[d], device_id={"nodes": peer}, device_id_type=MESH)
 
     def in_copy(g, d, slot):
         peer = ahead(d)
@@ -225,6 +245,10 @@
             return carry
 
         lax.fori_loop(1, count, step, 0)
+
+    def peers(act):
+        for d in order:
+            act(d)
 
     barrier = pltpu.get_barrier_semaphore()
     for d in range(1, nn):
@@ -232,34 +256,54 @@
     for d in range(1, rr):
         pl.semaphore_signal(barrier, inc=1, device_id={"rep": rep_ahead(d)}, device_id_type=MESH)
 
-    perm[...] = (
-        lax.broadcasted_iota(jnp.int32, (rows, rows), 0) == slot_row[...]
-    ).astype(jnp.float32).astype(low)
-    unperm[...] = (
-        lax.broadcasted_iota(jnp.int32, (rows, rows), 1) == slot_col[...]
-    ).astype(jnp.float32).astype(low)
-
-    gsend[:, :, :width] = dot(perm[...], g_ref[...]).astype(low).reshape(nn, bucket, width)
-    gsend[:, :, width:] = dot(perm[...], tags[...]).astype(low).reshape(nn, bucket, TAG_LANES)
+    ids = ids_ref[...]
+    owners = ids // CL_DEV
+    owner_table = jnp.where(
+        lax.broadcasted_iota(jnp.int32, (max(nn, 8), rows), 0) == owners, 1.0, 0.0)
+    tag_table = jnp.where(
+        lax.broadcasted_iota(jnp.int32, (TAG_ROWS, rows), 0) == ids - owners * CL_DEV, 1.0, 0.0)
+    down = lax.broadcasted_iota(jnp.int32, (rows, rows), 0)
+    across = lax.broadcasted_iota(jnp.int32, (rows, rows), 1)
+    before = dot(owner_table.astype(low), jnp.where(down < across, 1.0, 0.0).astype(low))
+    rank = jnp.sum(before * owner_table, axis=0, keepdims=True).astype(jnp.int32)
+    perm_wide = jnp.where(down == owners * bucket + rank, 1.0, 0.0)
+    perm[...] = perm_wide.astype(low)
+    gsend[...] = dot(perm[...], g_ref[...]).astype(low).reshape(nn, bucket, width)
     pl.semaphore_wait(barrier, nn + rr - 2)
-    each(nn, lambda d: g_copy(d, me).start())
+    peers(lambda d: g_copy(d, me).start())
     grecv[me] = gsend[me]
+    tag_line = dot_lanes(tag_table.astype(low), perm[...]).astype(low)
+    tall = lax.broadcasted_iota(jnp.int32, (rows, TAG_LANES), 0)
+    lane = lax.broadcasted_iota(jnp.int32, (rows, TAG_LANES), 1)
+    for o in range(nn):
+        pick = jnp.where((tall - lane == o * bucket) & (lane < bucket), 1.0, 0.0).astype(low)
+        tsend[o] = dot(tag_line, pick).astype(low)
+    peers(lambda d: t_copy(d, me).start())
+    trecv[me] = tsend[me]
 
     def perm_send(g):
         cols = pl.ds(pl.multiple_of(g * gcols, HEAD_DIM), gcols)
         for i, ref in enumerate((q_ref, k_ref, v_ref)):
             send[g, :, i] = dot(perm[...], ref[:, cols]).astype(low).reshape(nn, bucket, gcols)
-        each(nn, lambda d: in_copy(g, d, me).start())
+        peers(lambda d: in_copy(g, d, me).start())
         recv[g, me] = send[g, me]
 
     perm_send(0)
     if groups > 1:
         perm_send(1)
-
-    each(nn, lambda d: g_copy(d, behind(d)).wait_recv())
-    ga[...] = dot(grecv[:, :, :width].reshape(rows, width), w_ref[...]).astype(low)
-    tag_rows = grecv[:, :, width:].reshape(rows, TAG_LANES)
-    bias[...] = jnp.where(dot_lanes(tag_rows, tag_rows) > 0.5, 0.0, big_negative)
+    unperm[...] = jnp.transpose(perm_wide).astype(low)
+    peers(lambda d: t_copy(d, behind(d)).wait_recv())
+    tag_all = jnp.zeros((TAG_ROWS, rows), jnp.float32)
+    high = lax.broadcasted_iota(jnp.int32, (TAG_LANES, rows), 0)
+    wide = lax.broadcasted_iota(jnp.int32, (TAG_LANES, rows), 1)
+    for o in range(nn):
+        place = jnp.where(wide - high == o * bucket, 1.0, 0.0).astype(low)
+        tag_all = tag_all + dot(trecv[o], place)
+    tag_all = tag_all.astype(low)
+    bias[...] = jnp.where(dot_rows(tag_all, tag_all) > 0.5, 0.0, big_negative)
+
+    peers(lambda d: g_copy(d, behind(d)).wait_recv())
+    ga[...] = dot(grecv[...].reshape(rows, width), w_ref[...]).astype(low)
 
     def rep_sum(g):
         each(rr, lambda d: w_copy(g, d, rep_behind(d)).wait_recv())
@@ -267,10 +311,10 @@
         for d in range(1, rr):
             total = total + wrecv[g, rep_behind(d)].astype(jnp.float32)
         nsend[g] = total.astype(low)
-        each(nn, lambda d: n_copy(g, d, me).start())
+        peers(lambda d: n_copy(g, d, me).start())
 
     def node_sum(g):
-        each(nn, lambda d: n_copy(g, d, behind(d)).wait_recv())
+        peers(lambda d: n_copy(g, d, behind(d)).wait_recv())
         total = nsend[g, me].astype(jnp.float32)
         for d in range(1, nn):
             total = total + nrecv[g, behind(d)].astype(jnp.float32)
@@ -278,7 +322,7 @@
         fsend[:, cols] = total.astype(low)
 
     def put_back(g):
-        each(nn, lambda d: back_copy(g, d, behind(d)).wait_recv())
+        peers(lambda d: back_copy(g, d, behind(d)).wait_recv())
         cols = pl.ds(pl.multiple_of(g * gcols, HEAD_DIM), gcols)
         for i, ref in enumerate((dq_ref, dk_ref, dv_ref)):
             ref[:, cols] = dot(unperm[...], brecv[g, :, i].reshape(rows, gcols)).astype(low)
@@ -288,7 +332,7 @@
         def _():
             perm_send(g + 2)
 
-        each(nn, lambda d: in_copy(g, d, behind(d)).wait_recv())
+        peers(lambda d: in_copy(g, d, behind(d)).wait_recv())
         for h in range(gcols // HEAD_DIM):
             hc = slice(h * HEAD_DIM, (h + 1) * HEAD_DIM)
             q = recv[g, :, 0, :, hc].reshape(rows, HEAD_DIM)
@@ -308,9 +352,9 @@
             bsend[g, :, 0, :, hc] = dot(ds, k).astype(low).reshape(shape)
             bsend[g, :, 1, :, hc] = dot_rows(ds, q).astype(low).reshape(shape)
             bsend[g, :, 2, :, hc] = dot_rows(probs_low, gr).astype(low).reshape(shape)
-        each(nn, lambda d: back_copy(g, d, me).start())
+        peers(lambda d: back_copy(g, d, me).start())
         brecv[g, me] = bsend[g, me]
-        share = dot_rows(grecv[:, :, :width].reshape(rows, width), att[...]) * norm_factor
+        share = dot_rows(grecv[...].reshape(rows, width), att[...]) * norm_factor
         share = share.astype(low).reshape(nn, rr, seg, gcols)
         for r in range(rr):
             wsend[g, r] = share[:, r]
@@ -341,14 +385,15 @@
     put_back(groups - 1)
     frecv[mr] = fsend[...]
     each(rr, lambda d: f_copy(d, rep_behind(d)).wait_recv())
-    dw_ref[...] = frecv[...].reshape(rr * seg, width).astype(jnp.float32)
-
-    each(nn, lambda d: g_copy(d, me).wait_send())
+    dw_ref[...] = frecv[...].reshape(rr * seg, width)
+
+    peers(lambda d: g_copy(d, me).wait_send())
+    peers(lambda d: t_copy(d, me).wait_send())
 
     def drain(g, carry):
-        each(nn, lambda d: in_copy(g, d, me).wait_send())
-        each(nn, lambda d: back_copy(g, d, me).wait_send())
-        each(nn, lambda d: n_copy(g, d, me).wait_send())
+        peers(lambda d: in_copy(g, d, me).wait_send())
+        peers(lambda d: back_copy(g, d, me).wait_send())
+        peers(lambda d: n_copy(g, d, me).wait_send())
         each(rr, lambda d: w_copy(g, d, mr).wait_send())
         return carry
 
@@ -366,30 +411,21 @@
     seg = width // (nn * rr)
     norm_factor = 1.0 / math.sqrt(rr * nn * rows)
     low = jnp.bfloat16
-    ids = cluster_id[0]
-    owners = ids // CL_DEV
-    subs = ids - owners * CL_DEV
-    table = owners[:, None] == jnp.arange(nn, dtype=jnp.int32)[None, :]
-    number = jnp.arange(rows, dtype=jnp.int32)
-    earlier = (number[:, None] > number[None, :]).astype(low)
-    before = jnp.dot(earlier, table.astype(low), preferred_element_type=jnp.float32)
-    rank = jnp.sum(jnp.where(table, before, 0.0), axis=1).astype(jnp.int32)
-    slot = owners * bucket + rank
-    tags = (subs[:, None] == jnp.arange(TAG_LANES, dtype=jnp.int32)[None, :]).astype(low)
     vmem = pl.BlockSpec(memory_space=pltpu.VMEM)
     dma = pltpu.SemaphoreType.DMA
-    ext = width + TAG_LANES
     outs = pl.pallas_call(
         functools.partial(layer_kernel, nn, rr, groups, norm_factor),
         out_shape=[jax.ShapeDtypeStruct((rows, width), low)] * 3
-        + [jax.ShapeDtypeStruct((rr * seg, width), jnp.float32)],
-        in_specs=[vmem] * 8,
+        + [jax.ShapeDtypeStruct((rr * seg, width), low)],
+        in_specs=[vmem] * 6,
         out_specs=[vmem] * 4,
         scratch_shapes=[
             pltpu.VMEM((rows, rows), low),
             pltpu.VMEM((rows, rows), low),
-            pltpu.VMEM((nn, bucket, ext), low),
-            pltpu.VMEM((nn, bucket, ext), low),
+            pltpu.VMEM((nn, bucket, width), low),
+            pltpu.VMEM((nn, bucket, width), low),
+            pltpu.VMEM((nn, TAG_ROWS, TAG_LANES), low),
+            pltpu.VMEM((nn, TAG_ROWS, TAG_LANES), low),
             pltpu.VMEM((groups, nn, 3, bucket, gcols), low),
             pltpu.VMEM((groups, nn, 3, bucket, gcols), low),
             pltpu.VMEM((rows, width), low),
@@ -404,6 +440,7 @@
             pltpu.VMEM((seg, width), low),
             pltpu.VMEM((rr, seg, width), low),
             dma((nn,)), dma((nn,)),
+            dma((nn,)), dma((nn,)),
             dma((groups, nn)), dma((groups, nn)),
             dma((groups, nn)), dma((groups, nn)),
             dma((groups, rr)), dma((groups, rr)),
@@ -413,17 +450,18 @@
         compiler_params=pltpu.CompilerParams(
             collective_id=0, has_side_effects=True, vmem_limit_bytes=56 * 1024 * 1024
         ),
-    )(slot[None, :], slot[:, None], tags, queries[0], keys[0], values[0], grad_out[0], w_out)
-    return (outs[0][None], outs[1][None], outs[2][None], outs[3])
+    )(cluster_id, queries[0], keys[0], values[0], grad_out[0], w_out)
+    return (outs[0][None], outs[1][None], outs[2][None], outs[3].astype(jnp.float32))
 
 
 def local(queries, keys, values, grad_out, w_out, cluster_id):
     nn, rr = lax.axis_size("nodes"), lax.axis_size("rep")
     rows, width = queries.shape[1:]
     heads = width // HEAD_DIM
+    bucket_fits = rows // nn <= TAG_LANES
     fits = (
         rows % (16 * nn) == 0 and width % (16 * nn * rr) == 0 and heads % GROUP_HEADS == 0
-        and CL_DEV <= TAG_LANES and nn > 1 and rr > 1
+        and CL_DEV <= TAG_ROWS and bucket_fits and nn > 1 and rr > 1
     )
     chosen = local_kernel if fits else local_plain
     return chosen(queries, keys, values, grad_out, w_out, cluster_id)

time: 202 us -> 193 us (0.955)
  Pallas kernels: 191 us -> 186 us
    pallas_call x1, Pallas kernels: 191 us -> 186 us  [local_kernel(): pl.pallas_call(functools.partial(layer_kernel, nn, rr, groups, norm_facto...]
    add x2 -> x0, other arithmetic: 2.15 us -> none  [local_kernel(): slot = owners * bucket + rank]
    unnamed x10 -> x7, local copies, waits for them, and re-layouts: 5.15 us -> 4.3 us
where the time goes in v1:
time: 193 us; the launch traced here: 192 us
  Pallas kernels  186 us (96%)
  local copies, waits for them, and re-layouts  4.3 us (2%)
    pallas_call x1, Pallas kernels, local_kernel(): pl.pallas_call(functools.partial(layer_kernel, nn, rr, groups, norm_facto...  186 us
    unnamed x7, local copies, waits for them, and re-layouts  4.3 us

profile of v1, /device:TPU:1, one launch (start us, length us, event | category | flops | bytes accessed | tf_op | source)
XLA Modules:
  0.0 192.5 jit_solution(14492326962621794000)
XLA Ops:
  0.6 185.6 %shard_map.93 = (bf16[512,1024]{1,0:T(8,128)(2,1)}, bf16[512,1024]{1,0:T(8,128)(2,1)}, bf16[512,1024]{1,0:T(8,128)(2,1)}, bf16[128,1024]{1,0:T(8,128)(2,1)}) custom-call(s32[1,512]{1,0:T(1,128)} %ids_ref.1, bf16[512,1024]{1,0:T(8,128)(2,1)} %bitcast.10, bf16[512,1024]{1,0:T(8,128)(2,1)} %bitcast.11, bf16[512,1024]{1,0:T(8,128)(2,1)} %bitcast.12, ...), custom_call_target="tpu_custom_call" | custom-call | tf_op jit(solution)/shard_map/pallas_call | solution.py:416
  186.3 0.0 copy-start.1
  186.3 1.9 convert_element_type.3
  188.2 0.0 copy-start
  188.2 2.4 %copy.13 = bf16[1,512,1024]{2,1,0:T(8,128)(2,1)} copy(bf16[1,512,1024]{2,1,0:T(8,128)(2,1)} %bitcast.9) | data formatting | bytes 2097152
  190.5 0.0 copy-done.1
  190.5 1.0 copy.14
  191.5 0.0 copy-done
  191.5 1.0 copy.15
Async XLA Ops:
  186.3 4.2 %copy-start.1 = (bf16[512,1024]{1,0:T(8,128)(2,1)S(1)}, bf16[512,1024]{1,0:T(8,128)(2,1)}, u32[]{:S(2)}) copy-start(bf16[512,1024]{1,0:T(8,128)(2,1)} %get-tuple-element.9) | copy-start | bytes 3145732
  188.2 3.3 %copy-start = (bf16[512,1024]{1,0:T(8,128)(2,1)S(1)}, bf16[512,1024]{1,0:T(8,128)(2,1)}, u32[]{:S(2)}) copy-start(bf16[512,1024]{1,0:T(8,128)(2,1)} %get-tuple-element.10) | copy-start | bytes 3145732

commit v2 on v1

--- a/solution.py
+++ b/solution.py
@@ -158,9 +158,9 @@
 
 def layer_kernel(
     nn, rr, groups, norm_factor,
-    ids_ref, q_ref, k_ref, v_ref, g_ref, w_ref,
+    ids_ref, q_any, k_any, v_any, g_any, w_any,
     dq_ref, dk_ref, dv_ref, dw_ref,
-    perm, unperm, gsend, grecv, tsend, trecv, send, recv, ga, bias, att, bsend, brecv,
+    q_ref, k_ref, v_ref, g_ref, w_ref, load_sem, perm, unperm, gsend, grecv, tsend, trecv, send, recv, ga, bias, att, bsend, brecv,
     wsend, wrecv, nsend, nrecv, fsend, frecv,
     g_ss, g_rs, t_ss, t_rs, in_ss, in_rs, b_ss, b_rs, w_ss, w_rs, n_ss, n_rs, f_ss, f_rs,
 ):
@@ -255,6 +255,14 @@
         pl.semaphore_signal(barrier, inc=1, device_id={"nodes": ahead(d)}, device_id_type=MESH)
     for d in range(1, rr):
         pl.semaphore_signal(barrier, inc=1, device_id={"rep": rep_ahead(d)}, device_id_type=MESH)
+
+    loads = [
+        pltpu.make_async_copy(src, dst, load_sem.at[i])
+        for i, (src, dst) in enumerate((
+            (g_any, g_ref), (q_any, q_ref), (k_any, k_ref), (v_any, v_ref), (w_any, w_ref)))
+    ]
+    for load in loads:
+        load.start()
 
     ids = ids_ref[...]
     owners = ids // CL_DEV
@@ -268,6 +276,7 @@
     rank = jnp.sum(before * owner_table, axis=0, keepdims=True).astype(jnp.int32)
     perm_wide = jnp.where(down == owners * bucket + rank, 1.0, 0.0)
     perm[...] = perm_wide.astype(low)
+    loads[0].wait()
     gsend[...] = dot(perm[...], g_ref[...]).astype(low).reshape(nn, bucket, width)
     pl.semaphore_wait(barrier, nn + rr - 2)
     peers(lambda d: g_copy(d, me).start())
@@ -288,6 +297,8 @@
         peers(lambda d: in_copy(g, d, me).start())
         recv[g, me] = send[g, me]
 
+    for load in loads[1:]:
+        load.wait()
     perm_send(0)
     if groups > 1:
         perm_send(1)
@@ -417,9 +428,11 @@
         functools.partial(layer_kernel, nn, rr, groups, norm_factor),
         out_shape=[jax.ShapeDtypeStruct((rows, width), low)] * 3
         + [jax.ShapeDtypeStruct((rr * seg, width), low)],
-        in_specs=[vmem] * 6,
+        in_specs=[vmem] + [pl.BlockSpec(memory_space=pl.ANY)] * 5,
         out_specs=[vmem] * 4,
-        scratch_shapes=[
+        scratch_shapes=[pltpu.VMEM((rows, width), low)] * 4 + [
+            pltpu.VMEM((width, width), low),
+            dma((5,)),
             pltpu.VMEM((rows, rows), low),
             pltpu.VMEM((rows, rows), low),
             pltpu.VMEM((nn, bucket, width), low),

time: 193 us -> 191 us (0.990)
  Pallas kernels: 186 us -> 184 us
where the time goes in v2:
time: 191 us
  Pallas kernels  184 us (96%)
  local copies, waits for them, and re-layouts  4.3 us (2%)
    pallas_call x1, Pallas kernels, local_kernel(): pl.pallas_call(functools.partial(layer_kernel, nn, rr, groups, norm_facto...  184 us
    unnamed x7, local copies, waits for them, and re-layouts  4.3 us

profile of v2, /device:TPU:1, one launch (start us, length us, event | category | flops | bytes accessed | tf_op | source)
XLA Modules:
  0.0 191.0 jit_solution(14684795558736283903)
XLA Ops:
  0.6 184.2 %shard_map.93 = (bf16[512,1024]{1,0:T(8,128)(2,1)}, bf16[512,1024]{1,0:T(8,128)(2,1)}, bf16[512,1024]{1,0:T(8,128)(2,1)}, bf16[128,1024]{1,0:T(8,128)(2,1)}) custom-call(s32[1,512]{1,0:T(1,128)} %ids_ref.1, bf16[512,1024]{1,0:T(8,128)(2,1)} %bitcast.10, bf16[512,1024]{1,0:T(8,128)(2,1)} %bitcast.11, bf16[512,1024]{1,0:T(8,128)(2,1)} %bitcast.12, ...), custom_call_target="tpu_custom_call" | custom-call | tf_op jit(solution)/shard_map/pallas_call | solution.py:427
  184.8 0.0 copy-start.1
  184.8 1.9 convert_element_type.3
  186.7 0.0 copy-start
  186.7 2.4 %copy.13 = bf16[1,512,1024]{2,1,0:T(8,128)(2,1)} copy(bf16[1,512,1024]{2,1,0:T(8,128)(2,1)} %bitcast.9) | data formatting | bytes 2097152
  189.0 0.0 copy-done.1
  189.0 1.0 copy.14
  190.0 0.0 copy-done
  190.0 1.0 copy.15
Async XLA Ops:
  184.8 4.2 %copy-start.1 = (bf16[512,1024]{1,0:T(8,128)(2,1)S(1)}, bf16[512,1024]{1,0:T(8,128)(2,1)}, u32[]{:S(2)}) copy-start(bf16[512,1024]{1,0:T(8,128)(2,1)} %get-tuple-element.9) | copy-start | bytes 3145732
  186.7 3.3 %copy-start = (bf16[512,1024]{1,0:T(8,128)(2,1)S(1)}, bf16[512,1024]{1,0:T(8,128)(2,1)}, u32[]{:S(2)}) copy-start(bf16[512,1024]{1,0:T(8,128)(2,1)} %get-tuple-element.10) | copy-start | bytes 3145732
